TPU v7x, 256 devices: a whole 4x4x8 slice. The times are simulated.
256 devices in a mesh: section: 4 (over z_lo), seq: 64 (over x, y, z_hi, core).
Axes of the slice: x: 4, y: 4, z: 8 (z_hi: 2, z_lo: 4; z = z_hi * 4 + z_lo), core: 2. Of those that a mesh axis runs over, the one named last changes fastest.
Arguments:
- tokens: bfloat16 [65536, 1024], P('seq'), may hold values from -8 to 8
- enc_gain: float32 [1024], replicated, may hold values from 0.1 to 1.9
- w_query: bfloat16 [1024, 1024], P(None, 'section'), may hold values from -8 to 8
- w_key: bfloat16 [1024, 1024], P(None, 'section'), may hold values from -8 to 8
- w_value: bfloat16 [1024, 1024], P(None, 'section'), may hold values from -0.1875 to 0.1875
- w_out: bfloat16 [1024, 1024], P('section'), may hold values from -0.1875 to 0.1875
- neighbours: int32 [512, 8], P('seq'), may hold values from 0 to 511, as said below
- counts: int32 [512], P('seq'), may hold values from 3 to 8, as said below
- stain_of_section: int32 [4], P('section'), may hold values from 0 to 2, as said below
- stain_gain: float32 [3, 1024], replicated, may hold values from 0.1 to 1.9
- stain_weight: bfloat16 [3, 1024, 768], replicated, may hold values from -0.1875 to 0.1875
Outputs:
- patches: bfloat16 [4, 65536, 768], P('section', 'seq')
Inputs may be any that keep to these rules, and one draw needn't show every extreme that they name: neighbours[i, j] names a block held by the same index of seq as block i or by the index before or after it; slot 0 is block i itself, slot 1 a block of the index before (block 0 on the first), slot 2 a block of the index after (the last block on the last). `counts`: some block uses all 8 slots. `stain_of_section`: every stain is named by some section.
All inputs are finite; a program needn't handle non-finite values.
Results may differ from a plain program's by a relative error of at most 0.019.
Values may be sent and summed in bfloat16 or wider, within the bound.
A program may use at most 128 MiB of HBM per device.

v0:
```python
import jax
import jax.numpy as jnp
from jax import lax
from jax.sharding import PartitionSpec as P

HEAD_DIM = 64
BLOCK = 128
NEIGH = 8


def with_halo(cells, sides, width):
    for axis, dim in sides:
        count = lax.axis_size(axis)
        ends = count - 1
        head = lax.slice_in_dim(cells, 0, width, axis=dim)
        tail = lax.slice_in_dim(cells, cells.shape[dim] - width, cells.shape[dim], axis=dim)
        cells = jnp.concatenate(
            [
                lax.ppermute(tail, axis, [(i, (i + 1) % count) for i in range(ends)]),
                cells,
                lax.ppermute(head, axis, [((i + 1) % count, i) for i in range(ends)]),
            ],
            axis=dim,
        )
    return cells


def rms_norm(values, gain):
    values = values.astype(jnp.float32)
    return values * lax.rsqrt(jnp.mean(values * values, axis=-1, keepdims=True) + 1e-05) * gain


def per_device(
    tokens,
    enc_gain,
    w_query,
    w_key,
    w_value,
    w_out,
    neighbours,
    counts,
    stain_of_section,
    stain_gain,
    stain_weight,
):
    normed = rms_norm(tokens, enc_gain).astype(jnp.bfloat16)
    queries = jnp.dot(normed, w_query, preferred_element_type=jnp.float32).astype(jnp.bfloat16)
    keys = jnp.dot(normed, w_key, preferred_element_type=jnp.float32).astype(jnp.bfloat16)
    values = jnp.dot(normed, w_value, preferred_element_type=jnp.float32).astype(jnp.bfloat16)
    tok_rows = tokens.shape[0]
    local_blocks = tok_rows // BLOCK
    local_heads = queries.shape[1] // HEAD_DIM
    keys_values = jnp.stack([keys, values])
    widened = with_halo(keys_values, (("seq", 1),), tok_rows)
    anchor = (lax.axis_index("seq") - 1) * local_blocks
    local_ids = neighbours - anchor
    stored = widened.reshape(2, 3 * local_blocks, BLOCK, local_heads, HEAD_DIM)
    picked = stored[:, local_ids].reshape(2, local_blocks, NEIGH * BLOCK, local_heads, HEAD_DIM)
    query_blocks = queries.reshape(local_blocks, BLOCK, local_heads, HEAD_DIM)
    scores = (
        jnp.einsum("nqhd,nkhd->nhqk", query_blocks, picked[0], preferred_element_type=jnp.float32)
        * 0.125
    )
    valid = jnp.arange(NEIGH * BLOCK, dtype=jnp.int32)[None, :] // BLOCK < counts[:, None]
    scores = jnp.where(valid[:, None, None, :], scores, -1e30)
    top = jnp.max(scores, axis=-1, keepdims=True)
    expo = jnp.exp(scores - top)
    weights = (expo / jnp.sum(expo, axis=-1, keepdims=True)).astype(jnp.bfloat16)
    attended = jnp.einsum(
        "nhqk,nkhd->nqhd", weights, picked[1], preferred_element_type=jnp.float32
    ).astype(jnp.bfloat16)
    attended = attended.reshape(tok_rows, local_heads * HEAD_DIM)
    partial_value = jnp.dot(attended, w_out, preferred_element_type=jnp.float32)
    total = lax.psum(partial_value.astype(jnp.bfloat16), "section").astype(jnp.float32)
    encoded = (tokens.astype(jnp.float32) + total).astype(jnp.bfloat16)
    stain = stain_of_section[0]
    decoded = rms_norm(encoded, stain_gain[stain]).astype(jnp.bfloat16)
    chosen = lax.dynamic_index_in_dim(stain_weight, stain, 0, False)
    patches = jnp.dot(decoded, chosen, preferred_element_type=jnp.float32).astype(jnp.bfloat16)
    return patches[None]


def solution(mesh):
    placed = (
        P("seq", None),
        P(),
        P(None, "section"),
        P(None, "section"),
        P(None, "section"),
        P("section", None),
        P("seq", None),
        P("seq"),
        P("section"),
        P(),
        P(),
    )
    return jax.shard_map(
        per_device, mesh=mesh, in_specs=placed, out_specs=P("section", "seq", None), check_vma=False
    )
```

profile of v0, /device:TPU:1, one launch (start us, length us, event | category | flops | bytes accessed | tf_op | source)
XLA Modules:
  0.0 281.7 jit_solution(6167845986850702582)
XLA Ops:
  6.5 0.0 copy-start
  6.5 0.0 copy-start.1
  6.5 0.0 copy-start.7
  6.5 0.0 all-reduce.2.cloned.1.call-start
  6.5 0.0 copy-start.6
  6.6 2.2 fusion.11
  8.8 2.5 fusion.30
  11.3 0.0 copy-done.1
  11.3 0.0 copy-done.7
  11.3 0.0 copy-done.6
  11.3 0.0 copy-start.4
  11.3 0.8 fusion.31
  12.1 0.0 copy-start.3
  12.1 0.8 copy-done.3
  12.9 0.0 copy-start.5
  12.9 1.1 pad_maximum_fusion.1
  13.9 10.2 %collective-permute-start = (bf16[2,1024,256]{2,1,0:T(8,128)(2,1)}, bf16[2,1024,256]{2,1,0:T(8,128)(2,1)}, u32[]{:S(2)}, u32[]{:S(2)}) collective-permute-start(bf16[2,1024,256]{2,1,0:T(8,128)(2,1)} %pad_maximum_fusion.1), channel_id=1, source_target_pairs={{0,1},{1,2},{2,3},{3,4},{4,5},{5,6},{6,7},{7,8},{8,9},{9,10},{10,1... | collective-permute-start | bytes 3145736 | tf_op jit(solution)/shard_map/ppermute | solution.py:19
  24.1 1.9 collective-permute-start.1
  26.1 0.0 copy-done.4
  26.1 0.1 reshape.98
  26.2 2.6 convolution_convert_fusion.1
  28.8 2.8 reshape.107
  31.6 0.0 copy-done.5
  31.6 0.1 broadcast_compare_fusion
  31.7 6.7 %collective-permute-done = bf16[2,1024,256]{2,1,0:T(8,128)(2,1)} collective-permute-done((bf16[2,1024,256]{2,1,0:T(8,128)(2,1)}, bf16[2,1024,256]{2,1,0:T(8,128)(2,1)}, u32[]{:S(2)}, u32[]{:S(2)}) %collective-permute-start) | collective-permute-done | bytes 1048608 | tf_op jit(solution)/shard_map/ppermute | solution.py:19
  38.4 20.4 %collective-permute-done.1 = bf16[2,1024,256]{2,1,0:T(8,128)(2,1)} collective-permute-done((bf16[2,1024,256]{2,1,0:T(8,128)(2,1)}, bf16[2,1024,256]{2,1,0:T(8,128)(2,1)}, u32[]{:S(2)}, u32[]{:S(2)}) %collective-permute-start.1) | collective-permute-done | bytes 1048608 | tf_op jit(solution)/shard_map/ppermute | solution.py:21
  58.8 3.1 %pad_maximum_fusion = bf16[2,3072,256]{2,1,0:T(8,128)(2,1)} fusion(bf16[2,1024,256]{2,1,0:T(8,128)(2,1)} %collective-permute-done.1, bf16[1,1024,256]{2,1,0:T(8,128)(2,1)} %copy-done.3, bf16[1,1024,256]{2,1,0:T(8,128)(2,1)S(1)} %fusion.30, bf16[2,1024,256]{2,1,0:T(8,128)(2,1)} %collective-permute-done), kind=kLoop, calls=%fused_computation.24 | loop fusion | flops 12582912 | bytes 6291456 | tf_op jit(solution)/shard_map/concatenate | solution.py:17
  61.9 10.2 %reshape.106 = bf16[2,24,128,4,64]{4,3,2,1,0:T(4,128)(2,1)} reshape(bf16[2,3072,256]{2,1,0:T(8,128)(2,1)} %pad_maximum_fusion) | data formatting | bytes 6291456 | tf_op jit(solution)/shard_map/reshape | solution.py:57
  72.1 9.5 %copy.20 = bf16[2,24,128,4,64]{2,4,3,1,0:T(8,128)(2,1)} copy(bf16[2,24,128,4,64]{4,3,2,1,0:T(4,128)(2,1)} %reshape.106) | data formatting | bytes 6291456 | tf_op jit(solution)/shard_map/reshape | solution.py:57
  81.6 7.4 %gather_fusion = bf16[64,2,128,4,64]{2,4,3,1,0:T(8,128)(2,1)} fusion(bf16[2,24,128,4,64]{2,4,3,1,0:T(8,128)(2,1)} %copy.20, s32[1024]{0:T(1024)S(1)} %pad_clamp_fusion), kind=kCustom, calls=%fused_computation | custom fusion | bytes 16777472 | tf_op jit(solution)/shard_map/gather | solution.py:58
  89.0 23.7 %copy.47 = bf16[8,8,2,128,4,64]{3,1,5,4,0,2:T(8,128)(2,1)} copy(bf16[8,8,2,128,4,64]{3,5,4,2,1,0:T(8,128)(2,1)} %bitcast.44) | data formatting | bytes 16777216 | tf_op jit(solution)/shard_map/gather | solution.py:58
  112.7 5.9 %fusion.52 = (bf16[1,8,8,128,4,64]{3,2,5,4,1,0:T(8,128)(2,1)}, bf16[1,8,8,128,4,64]{3,2,5,4,1,0:T(8,128)(2,1)}) fusion(bf16[2,8,8,128,4,64]{3,2,5,4,1,0:T(8,128)(2,1)} %bitcast.45), kind=kLoop, calls=%fused_computation.62 | loop fusion | bytes 16777216 | tf_op jit(solution)/shard_map/slice | solution.py:61
  118.6 7.3 %squeeze.14 = bf16[8,1024,4,64]{1,3,2,0:T(8,128)(2,1)} reshape(bf16[1,8,8,128,4,64]{3,2,5,4,1,0:T(8,128)(2,1)} %get-tuple-element.5) | data formatting | bytes 8388608 | tf_op jit(solution)/shard_map/squeeze | solution.py:61
  125.9 7.3 %squeeze.13 = bf16[8,1024,4,64]{1,3,2,0:T(8,128)(2,1)} reshape(bf16[1,8,8,128,4,64]{3,2,5,4,1,0:T(8,128)(2,1)} %get-tuple-element.6) | data formatting | bytes 8388608 | tf_op jit(solution)/shard_map/squeeze | solution.py:70
  133.2 10.7 %fusion.53 = (f32[8,4,128]{2,1,0:T(4,128)S(1)}, f32[8,4,128,1024]{3,2,1,0:T(8,128)}) fusion(pred[8,1024]{1,0:T(8,128)(4,1)S(1)} %broadcast_compare_fusion, bf16[8,1024,4,64]{1,3,2,0:T(8,128)(2,1)} %squeeze.14, bf16[8,128,4,64]{3,2,1,0:T(4,128)(2,1)} %reshape.107), kind=kOutput, calls=%fused_computation.63 | convolution fusion | flops 553649152 | bytes 21520384 | tf_op jit(solution)/shard_map/sub | solution.py:67
  143.9 10.1 %fusion.32 = bf16[8,128,4,64]{1,3,2,0:T(8,128)(2,1)S(1)} fusion(bf16[8,1024,4,64]{1,3,2,0:T(8,128)(2,1)} %squeeze.13, f32[8,4,128,1024]{3,2,1,0:T(8,128)} %get-tuple-element.8, f32[8,4,128]{2,1,0:T(4,128)S(1)} %get-tuple-element.7), kind=kOutput, calls=%fused_computation.39 | convolution fusion | flops 545521664 | bytes 21512192 | tf_op jit(solution)/shard_map/nhqk,nkhd->nqhd/dot_general | solution.py:69
  154.0 0.3 copy.24
  154.4 0.0 copy-done
  154.4 2.1 convolution_convert_fusion
  156.5 0.0 all-reduce.2.cloned.1.call-update
  157.1 0.7 constant_dynamic-slice_fusion
  157.9 109.8 %all-reduce.2.cloned.1.call-done = bf16[1024,1024]{1,0:T(8,128)(2,1)} async-done(((bf16[1024,1024]{1,0:T(8,128)(2,1)}), bf16[1024,1024]{1,0:T(8,128)(2,1)}) %all-reduce.2.cloned.1.call-update) | async-done | bytes 2097168 | tf_op jit(solution)/shard_map/psum | solution.py:74
  267.7 0.0 copy-start.2
  267.7 2.5 fusion.8
  270.2 0.0 copy-done.2
  270.2 4.6 %fusion.24 = bf16[1,1024,768]{2,1,0:T(8,128)(2,1)} fusion(bf16[3,1024,768]{2,1,0:T(8,128)(2,1)} %param.21, s32[]{:T(128)S(6)} %select_n.25, f32[1024]{0:T(1024)S(1)} %bitcast.47, f32[1024]{0:T(1024)S(1)} %add_rsqrt_fusion, bf16[1024,1024]{1,0:T(8,128)(2,1)S(1)} %copy-done.1, bf16[1024,1024]{1,0:T(8,128)(2,1)S(1)} %copy-done.2), kind=kOutput, calls=%fused_computation.32 | convolution fusion | flops 1619787776 | bytes 7348228 | tf_op jit(solution)/shard_map/dot_general | solution.py:79
  (5 shorter events, 0.0 us)
Async XLA Ops:
  6.5 147.9 %copy-start = (bf16[256,1024]{1,0:T(8,128)(2,1)S(1)}, bf16[256,1024]{1,0:T(8,128)(2,1)}, u32[]{:S(2)}) copy-start(bf16[256,1024]{1,0:T(8,128)(2,1)} %param.16) | copy-start | bytes 1572868
  6.5 4.7 %copy-start.1 = (bf16[1024,1024]{1,0:T(8,128)(2,1)S(1)}, bf16[1024,1024]{1,0:T(8,128)(2,1)}, u32[]{:S(2)}) copy-start(bf16[1024,1024]{1,0:T(8,128)(2,1)} %param.11) | copy-start | bytes 6291460
  6.5 4.7 %copy-start.7 = (f32[1024]{0:T(1024)S(1)}, f32[1024]{0:T(1024)}, u32[]{:S(2)}) copy-start(f32[1024]{0:T(1024)} %param.12) | copy-start | bytes 12292
  6.5 261.2 %all-reduce.2.cloned.1.call-start = ((), (), s32[]{:S(2)}) async-start(), calls=%async_computation | async-start | bytes 4194304 | tf_op jit(solution)/shard_map/psum | solution.py:74
  6.5 4.7 %copy-start.6 = (bf16[1024,256]{1,0:T(8,128)(2,1)S(1)}, bf16[1024,256]{1,0:T(8,128)(2,1)}, u32[]{:S(2)}) copy-start(bf16[1024,256]{1,0:T(8,128)(2,1)} %param.15) | copy-start | bytes 1572868
  11.3 14.8 %copy-start.4 = (s32[8,8]{1,0:T(8,128)S(1)}, s32[8,8]{1,0:T(8,128)}, u32[]{:S(2)}) copy-start(s32[8,8]{1,0:T(8,128)} %param.17) | copy-start | bytes 772
  12.1 0.8 copy-start.3
  12.9 18.7 %copy-start.5 = (s32[8]{0:T(128)S(1)}, s32[8]{0:T(128)}, u32[]{:S(2)}) copy-start(s32[8]{0:T(128)} %param.18) | copy-start | bytes 100
  13.9 24.5 %collective-permute-start = (bf16[2,1024,256]{2,1,0:T(8,128)(2,1)}, bf16[2,1024,256]{2,1,0:T(8,128)(2,1)}, u32[]{:S(2)}, u32[]{:S(2)}) collective-permute-start(bf16[2,1024,256]{2,1,0:T(8,128)(2,1)} %pad_maximum_fusion.1), channel_id=1, source_target_pairs={{0,1},{1,2},{2,3},{3,4},{4,5},{5,6},{6,7},{7,8},{8,9},{9,10},{10,1... | collective-permute-start | bytes 3145736 | tf_op jit(solution)/shard_map/ppermute | solution.py:19
  24.1 34.6 %collective-permute-start.1 = (bf16[2,1024,256]{2,1,0:T(8,128)(2,1)}, bf16[2,1024,256]{2,1,0:T(8,128)(2,1)}, u32[]{:S(2)}, u32[]{:S(2)}) collective-permute-start(bf16[2,1024,256]{2,1,0:T(8,128)(2,1)} %pad_maximum_fusion.1), channel_id=1, source_target_pairs={{1,0},{2,1},{3,2},{4,3},{5,4},{6,5},{7,6},{8,7},{9,8},{10,9},{11,1... | collective-permute-start | bytes 3145736 | tf_op jit(solution)/shard_map/ppermute | solution.py:21
  267.7 2.5 copy-start.2
Sparse Core Ops, SparseCore 0:
  156.6 111.0 all-reduce.1
where the time goes:
time: 283 us; the launch traced here: 282 us
  waiting for transfers between devices  137 us (48%)
  local copies, waits for them, and re-layouts  76 us (27%)
  matrix products  33.3 us (12%)
  between operations  14.2 us (5%)
  starting transfers between devices  12.1 us (4%)
  other arithmetic  9.01 us (3%)
    psum x1, waiting for transfers between devices, per_device(): lax.psum(partial_value.astype(jnp.bfloat16), 'section').astype(jnp.float32)  110 us
    gather x2, local copies, waits for them, and re-layouts, per_device(): stored[:, local_ids]  31.1 us
    ppermute x1, waiting for transfers between devices, with_halo(): lax.ppermute(head, axis, [((i + 1) % count, i) for i in range(ends)])  20.4 us
    reshape x2, local copies, waits for them, and re-layouts, per_device(): stored = widened.reshape(2, 3 * local_blocks, BLOCK, local_heads, HEAD_DIM)  19.7 us
    sub x1, matrix products, per_device(): expo = jnp.exp(scores - top)  10.7 us
    ppermute x1, starting transfers between devices, with_halo(): lax.ppermute(tail, axis, [(i, (i + 1) % count) for i in range(ends)])  10.2 us
    dot_general x1, matrix products, per_device(): jnp.einsum('nhqk,nkhd->nqhd', weights, picked[1], preferred_element_type=...  10.1 us
    squeeze x1, local copies, waits for them, and re-layouts, per_device(): picked[0]  7.32 us
  transfers between devices with their start and end apart: 3, of which 3 were waited for; matrix products, arithmetic and copies ran while one was open for 2% of the time, Pallas kernels for 0%

commit v1 on v0

v1 whole, which is shorter than its diff:
```python
import functools

import jax
import jax.numpy as jnp
from jax import lax
from jax.experimental import pallas as pl
from jax.experimental.pallas import tpu as pltpu
from jax.sharding import PartitionSpec as P

HEAD_DIM = 64
BLOCK = 128
NEIGH = 8
TOK = 1024
WIDTH = 1024
PIX = 768
GROUP = 4
COLS = WIDTH // GROUP
CHUNK = 32
HALF = TOK // 2
CHUNKS = HALF // CHUNK
STEPS = CHUNKS + GROUP - 1
QSCALE = 0.125 * 1.4426950408889634

F32 = jnp.float32
BF16 = jnp.bfloat16
MESH = pl.DeviceIdType.MESH


def gather_project(
    tok_hbm, gain_ref, wq_hbm, wk_hbm, wv_hbm, wo_hbm,
    q_out, kv_out, wo_out,
    raw, norm, wts, q_buf, own_kv, halo_kv,
    tok_sem, wload_sem, lo_send, lo_recv, hi_send, hi_recv,
    z_send, z_recv, row_send, row_recv, col_send, col_recv, pair_send, pair_recv,
    kv_send, kv_recv, store_sem, hstore_sem,
):
    sec = lax.axis_index("section")
    seq = lax.axis_index("seq")
    core = seq % 2
    zhi = (seq // 2) % 2
    yy = (seq // 4) % 4
    xx = seq // 16
    u = xx * (1 - core) + yy * core
    v = yy * (1 - core) + xx * core

    def seq_at(u1, v1):
        x1 = u1 * (1 - core) + v1 * core
        y1 = v1 * (1 - core) + u1 * core
        return ((x1 * 4 + y1) * 2 + zhi) * 2 + core

    def z_at(step):
        z1 = (zhi * 4 + sec + step + 8) % 8
        return (z1 % 4, seq + (z1 // 4 - zhi) * 2)

    sibling = (sec, seq + 1 - 2 * core)
    partner = (seq + 2 * core - 1 + 64) % 64
    up, down = z_at(1), z_at(7)
    two_up, two_down = z_at(2), z_at(6)
    first = jnp.where(sec == 0, 1, 0)
    last = jnp.where(sec == 3, 1, 0)
    lo_to = ((sec + 3) % 4, jnp.where(sec == 0, partner, seq))
    hi_to = ((sec + 1) % 4, jnp.where(sec == 3, partner, seq))
    row_to = [(sec, seq_at((u + d) % 4, v)) for d in (1, 3, 2)]
    col_to = [(sec, seq_at(u, (v + d) % 4)) for d in (1, 3)]

    tok_loads = []
    for i in range(4):
        rows = pl.ds(i * 256, 256)
        tok_loads.append(pltpu.make_async_copy(tok_hbm.at[rows, :], raw.at[rows, :], tok_sem.at[i]))
    w_loads = [
        pltpu.make_async_copy(src, wts.at[0, i], wload_sem.at[i])
        for i, src in enumerate((wq_hbm, wk_hbm, wv_hbm))
    ]
    for i in range(4):
        w_loads.append(
            pltpu.make_async_copy(
                wo_hbm.at[:, pl.ds(i * COLS, COLS)],
                wts.at[0, 3, pl.ds(i * COLS, COLS), :],
                wload_sem.at[3 + i],
            )
        )
    for copy in tok_loads + w_loads:
        copy.start()

    barrier = pltpu.get_barrier_semaphore()
    peers = [sibling, up, down, two_up, two_down, lo_to, hi_to] + row_to + col_to
    for peer in peers:
        pl.semaphore_signal(barrier, inc=1, device_id=peer, device_id_type=MESH)

    gain = gain_ref[...]
    for i in range(4):
        tok_loads[i].wait()

        def norm_rows(t, _):
            rows = pl.ds(pl.multiple_of(i * 256 + t * 128, 128), 128)
            x = raw[rows, :].astype(F32)
            scale = lax.rsqrt(jnp.mean(x * x, axis=-1, keepdims=True) + 1e-05)
            norm[0, rows, :] = (x * scale * gain).astype(BF16)
            return 0

        lax.fori_loop(0, 2, norm_rows, 0)

    pl.semaphore_wait(barrier, len(peers))

    def remote(src, dst, send, recv, to):
        return pltpu.make_async_remote_copy(
            src_ref=src, dst_ref=dst, send_sem=send, recv_sem=recv, device_id=to, device_id_type=MESH
        )

    def lo_copy(j):
        rows = pl.ds(pl.multiple_of(j * CHUNK, CHUNK), CHUNK)
        return remote(norm.at[1 - first, rows, :], norm.at[1, rows, :], lo_send.at[j], lo_recv.at[j], lo_to)

    def hi_copy(j):
        rows = pl.ds(pl.multiple_of(HALF + j * CHUNK, CHUNK), CHUNK)
        return remote(norm.at[1 - last, rows, :], norm.at[1, rows, :], hi_send.at[j], hi_recv.at[j], hi_to)

    def start_lo(j, _):
        lo_copy(j).start()
        return 0

    def start_hi(j, _):
        hi_copy(j).start()
        return 0

    piece = pl.ds(pl.multiple_of(core * HALF + (v * 4 + u) * 32, 32), 32)

    def slab(g, rows):
        if g < 3:
            return wts.at[g + 1, pl.ds(0, 3), rows, :]
        return wts.at[pl.ds(1, 3), 3, rows, :]

    two_sec = jnp.where(core == 0, two_up[0], two_down[0])
    two_seq = jnp.where(core == 0, two_up[1], two_down[1])
    z_to = [down, (two_sec, two_seq), up]
    z_copies = [
        remote(wts.at[0, pl.ds(0, 3), piece, :], wts.at[r + 1, pl.ds(0, 3), piece, :], z_send.at[r], z_recv.at[r], z_to[r])
        for r in range(3)
    ] + [
        remote(wts.at[0, 3, piece, :], wts.at[r + 1, 3, piece, :], z_send.at[3 + r], z_recv.at[3 + r], z_to[r])
        for r in range(3)
    ]
    for copy in w_loads:
        copy.wait()
    for copy in z_copies:
        copy.start()

    @pl.when(sec == 0)
    def _():
        lax.fori_loop(0, CHUNKS, start_lo, 0)

    @pl.when(sec == 3)
    def _():
        lax.fori_loop(0, CHUNKS, start_hi, 0)

    def row_copy(g, d):
        return remote(slab(g, piece), slab(g, piece), row_send.at[g * 3 + d], row_recv.at[g * 3 + d], row_to[d])

    def set_rows(v1, start=0, size=128):
        return pl.ds(pl.multiple_of(core * HALF + v1 * 128 + start, 32), size)

    def col_copy(g, d):
        if d < 2:
            rows = set_rows(v)
        elif d == 2:
            rows = set_rows((v + 3) % 4, 0, 64)
        else:
            rows = set_rows((v + 1) % 4, 64, 64)
        return remote(slab(g, rows), slab(g, rows), col_send.at[g * 4 + d], col_recv.at[g * 4 + d], col_to[d % 2])

    def pair_copy(g, d):
        rows = set_rows((v + d) % 4)
        return remote(slab(g, rows), slab(g, rows), pair_send.at[g * 4 + d], pair_recv.at[g * 4 + d], sibling)

    def e1(g):
        if g < 3:
            z_copies[g].wait_recv()
        else:
            for r in range(3):
                z_copies[3 + r].wait_recv()
        for d in range(3):
            row_copy(g, d).start()

    def e3(g):
        for d in range(3):
            row_copy(g, d).wait_recv()
        for d in range(2):
            col_copy(g, d).start()
        pair_copy(g, 0).start()

    def e4(g):
        col_copy(g, 0).wait_recv()
        col_copy(g, 2).start()
        pair_copy(g, 3).start()
        col_copy(g, 1).wait_recv()
        col_copy(g, 3).start()
        pair_copy(g, 1).start()

    def e5(g):
        col_copy(g, 2).wait_recv()
        col_copy(g, 3).wait_recv()
        pair_copy(g, 2).start()

    def e6(g):
        for d in range(4):
            pair_copy(g, d).wait_recv()

    def halo_step(k):
        j = k - 3 + sec

        @pl.when((j >= 0) & (j < CHUNKS))
        def _():
            lo_copy(j).wait_recv()

            @pl.when(sec != 0)
            def _():
                lo_copy(j).start()

        i = k - sec

        @pl.when((i >= 0) & (i < CHUNKS))
        def _():
            hi_copy(i).wait_recv()

            @pl.when(sec != 3)
            def _():
                hi_copy(i).start()

    def own_unit(r, t):
        rows = pl.ds(pl.multiple_of(t * 256, 256), 256)
        x = norm[0, rows, :]
        q = jnp.dot(x, wts[r, 0], preferred_element_type=F32)
        q_buf[r, rows, :] = (q * QSCALE).astype(BF16)
        own_kv[r, 0, rows, :] = jnp.dot(x, wts[r, 1], preferred_element_type=F32).astype(BF16)
        own_kv[r, 1, rows, :] = jnp.dot(x, wts[r, 2], preferred_element_type=F32).astype(BF16)

    def halo_unit(m, r):
        low = pl.ds(pl.multiple_of(m * 128, 128), 128)
        high = pl.ds(pl.multiple_of(HALF + m * 128, 128), 128)
        x = jnp.concatenate([norm[1, low, :], norm[1, high, :]], axis=0)
        for w in range(2):
            y = jnp.dot(x, wts[r, 1 + w], preferred_element_type=F32).astype(BF16)
            halo_kv[w, r, low, :] = y[:128]
            halo_kv[w, r, high, :] = y[128:]

    def own_stores(r):
        return [
            pltpu.make_async_copy(q_buf.at[r], q_out.at[r], store_sem.at[r * 2]),
            pltpu.make_async_copy(own_kv.at[r], kv_out.at[:, r, pl.ds(0, TOK), :], store_sem.at[r * 2 + 1]),
        ]

    def kv_copy(r):
        return remote(own_kv.at[r], kv_out.at[:, r, pl.ds(2 * TOK, TOK), :], kv_send.at[r], kv_recv.at[r], sibling)

    def halo_stores(m):
        copies = []
        for h in range(2):
            copies.append(
                pltpu.make_async_copy(
                    halo_kv.at[:, :, pl.ds(h * HALF + m * 128, 128), :],
                    kv_out.at[:, :, pl.ds(TOK + h * HALF + m * 128, 128), :],
                    hstore_sem.at[m * 2 + h],
                )
            )
        return copies

    def finish_own(r):
        for copy in own_stores(r):
            copy.start()
        kv_copy(r).start()

    def run(first_step, last_step, events, unit):
        def body(k, _):
            halo_step(k)
            for at, event in events:
                pl.when(k == at)(event)
            unit(k)
            return 0

        lax.fori_loop(first_step, last_step + 1, body, 0)

    def seqn(*pairs):
        def go():
            for fn, g in pairs:
                fn(g)

        return go

    run(0, 3, [(1, seqn((e1, 0), (e1, 1))), (2, seqn((e1, 2), (e1, 3))), (3, seqn((e3, 0)))], lambda k: own_unit(0, k))
    finish_own(0)
    run(4, 6, [(4, seqn((e3, 1), (e3, 2))), (5, seqn((e3, 3), (e4, 0))), (6, seqn((e5, 0)))], lambda k: None)

    def unit_r1(k):
        own_unit(1, k - 7)

        @pl.when(k < 9)
        def _():
            halo_unit(0, k - 7)

    run(7, 10, [(7, seqn((e6, 0))), (8, seqn((e4, 1))), (9, seqn((e5, 1)))], unit_r1)
    finish_own(1)

    def unit_r2(k):
        own_unit(2, k - 11)
        t = k - 11
        halo_unit(1 - t // 3, t - t // 3)

    run(11, 14, [(11, seqn((e6, 1), (e4, 2))), (12, seqn((e5, 2))), (13, seqn((e4, 3))), (14, seqn((e5, 3)))], unit_r2)
    finish_own(2)

    def unit_r3(k):
        own_unit(3, k - 15)
        halo_unit(2, k - 15)

        @pl.when(k < 17)
        def _():
            halo_unit(k - 15, 3)

    run(15, STEPS - 1, [(15, seqn((e6, 2))), (16, seqn((e6, 3)))], unit_r3)
    finish_own(3)
    wo_store = pltpu.make_async_copy(wts.at[:, 3], wo_out, wload_sem.at[7])
    wo_store.start()
    for m in range(3):
        for copy in halo_stores(m):
            copy.start()

    def tail(r, _):
        halo_unit(3, r)
        return 0

    lax.fori_loop(0, GROUP, tail, 0)
    for copy in halo_stores(3):
        copy.start()

    def drain(j, _):
        lo_copy(j).wait_send()
        hi_copy(j).wait_send()
        return 0

    lax.fori_loop(0, CHUNKS, drain, 0)
    for copy in z_copies:
        copy.wait_send()
    for g in range(4):
        for d in range(3):
            row_copy(g, d).wait_send()
        for d in range(4):
            col_copy(g, d).wait_send()
            pair_copy(g, d).wait_send()
    for r in range(GROUP):
        for copy in own_stores(r):
            copy.wait()
        kv_copy(r).wait()
    wo_store.wait()
    for m in range(4):
        for copy in halo_stores(m):
            copy.wait()


def project(tokens, gain, wq, wk, wv, wo):
    any_spec = pl.BlockSpec(memory_space=pl.ANY)
    dma = pltpu.SemaphoreType.DMA
    return pl.pallas_call(
        gather_project,
        out_shape=[
            jax.ShapeDtypeStruct((GROUP, TOK, COLS), BF16),
            jax.ShapeDtypeStruct((2, GROUP, 3 * TOK, COLS), BF16),
            jax.ShapeDtypeStruct((GROUP, WIDTH, COLS), BF16),
        ],
        in_specs=[any_spec, pl.BlockSpec(memory_space=pltpu.VMEM)] + [any_spec] * 4,
        out_specs=[any_spec] * 3,
        scratch_shapes=[
            pltpu.VMEM((TOK, WIDTH), BF16),
            pltpu.VMEM((2, TOK, WIDTH), BF16),
            pltpu.VMEM((GROUP, 4, WIDTH, COLS), BF16),
            pltpu.VMEM((GROUP, TOK, COLS), BF16),
            pltpu.VMEM((GROUP, 2, TOK, COLS), BF16),
            pltpu.VMEM((2, GROUP, TOK, COLS), BF16),
            dma((4,)), dma((8,)),
            dma((CHUNKS,)), dma((CHUNKS,)), dma((CHUNKS,)), dma((CHUNKS,)),
            dma((6,)), dma((6,)), dma((12,)), dma((12,)), dma((16,)), dma((16,)), dma((16,)), dma((16,)),
            dma((4,)), dma((4,)), dma((8,)), dma((8,)),
        ],
        compiler_params=pltpu.CompilerParams(
            collective_id=0, has_side_effects=True, vmem_limit_bytes=52 * 2**20
        ),
        name="gather_project",
    )(tokens, gain, wq, wk, wv, wo)


PAIRS = 4


def attend_decode(
    ids_ref, counts_ref, stain_ref,
    q_ref, k_ref, v_ref, wo_ref, tok_ref, gain_ref, sw_ref,
    out_ref, att, e_scr,
):
    del stain_ref
    step = pl.program_id(0)
    lane = lax.broadcasted_iota(jnp.int32, (BLOCK, BLOCK), 1)

    def block(i, _):
        rows = pl.ds(pl.multiple_of(i * BLOCK, BLOCK), BLOCK)
        starts = [pl.multiple_of(ids_ref[i, j] * BLOCK, BLOCK) for j in range(NEIGH)]

        def run(n):
            for p in range(PAIRS):
                r, c = p // 2, (p % 2) * BLOCK
                q = q_ref[r, rows, c : c + BLOCK]
                zero = jnp.zeros_like(q)
                both = jnp.concatenate([jnp.where(lane < HEAD_DIM, q, zero), jnp.where(lane < HEAD_DIM, zero, q)], axis=0)
                k = jnp.concatenate([k_ref[0, r, pl.ds(starts[j], BLOCK), c : c + BLOCK] for j in range(n)], axis=0)
                s = lax.dot_general(both, k, (((1,), (1,)), ((), ())), preferred_element_type=F32)
                top = jnp.max(s, axis=1, keepdims=True)
                e_scr[p, :, : n * BLOCK] = jnp.exp2(s - top).astype(BF16)
            for p in range(PAIRS):
                r, c = p // 2, (p % 2) * BLOCK
                v = jnp.concatenate([v_ref[0, r, pl.ds(starts[j], BLOCK), c : c + BLOCK] for j in range(n)], axis=0)
                v = jnp.concatenate([v, jnp.ones((n * BLOCK, BLOCK), BF16)], axis=1)
                o = jnp.dot(e_scr[p, :, : n * BLOCK], v, preferred_element_type=F32)
                o = o[:, :BLOCK] / o[:, BLOCK:]
                att[step * 2 + r, rows, c : c + BLOCK] = jnp.where(lane < HEAD_DIM, o[:BLOCK], o[BLOCK:]).astype(BF16)

        for n in range(3, NEIGH + 1):
            pl.when(counts_ref[i] == n)(functools.partial(run, n))
        return 0

    lax.fori_loop(0, TOK // BLOCK, block, 0)

    @pl.when(step == GROUP // 2 - 1)
    def _():
        gain = gain_ref[0]

        def rows_out(t, _):
            rows = pl.ds(pl.multiple_of(t * 256, 256), 256)
            x = jnp.concatenate([att[r, rows, :] for r in range(GROUP)], axis=1)
            parts = []
            for c in range(GROUP):
                w = jnp.concatenate([wo_ref[r, c * COLS : (c + 1) * COLS, :] for r in range(GROUP)], axis=0)
                parts.append(jnp.dot(x, w, preferred_element_type=F32))
            mixed = jnp.concatenate(parts, axis=1)
            encoded = (tok_ref[rows, :].astype(F32) + mixed).astype(BF16).astype(F32)
            scale = lax.rsqrt(jnp.mean(encoded * encoded, axis=-1, keepdims=True) + 1e-05)
            decoded = (encoded * scale * gain).astype(BF16)
            out_ref[0, rows, :] = jnp.dot(decoded, sw_ref[0], preferred_element_type=F32).astype(BF16)
            return 0

        lax.fori_loop(0, 4, rows_out, 0)


def attention(ids, counts, stain, q, kv, wo, tokens, stain_gain, stain_weight):
    half = GROUP // 2
    return pl.pallas_call(
        attend_decode,
        out_shape=jax.ShapeDtypeStruct((1, TOK, PIX), BF16),
        grid_spec=pltpu.PrefetchScalarGridSpec(
            num_scalar_prefetch=3,
            grid=(2,),
            in_specs=[
                pl.BlockSpec((half, TOK, COLS), lambda g, *_: (g, 0, 0)),
                pl.BlockSpec((1, half, 3 * TOK, COLS), lambda g, *_: (0, g, 0, 0)),
                pl.BlockSpec((1, half, 3 * TOK, COLS), lambda g, *_: (1, g, 0, 0)),
                pl.BlockSpec((GROUP, WIDTH, COLS), lambda g, *_: (0, 0, 0), pipeline_mode=pl.Buffered(1)),
                pl.BlockSpec((TOK, WIDTH), lambda g, *_: (0, 0), pipeline_mode=pl.Buffered(1)),
                pl.BlockSpec((1, 1, WIDTH), lambda g, ids, counts, stain: (stain[0], 0, 0)),
                pl.BlockSpec((1, WIDTH, PIX), lambda g, ids, counts, stain: (stain[0], 0, 0), pipeline_mode=pl.Buffered(1)),
            ],
            out_specs=pl.BlockSpec((1, TOK, PIX), lambda g, *_: (0, 0, 0)),
            scratch_shapes=[
                pltpu.VMEM((GROUP, TOK, COLS), BF16),
                pltpu.VMEM((PAIRS, 2 * BLOCK, NEIGH * BLOCK), BF16),
            ],
        ),
        compiler_params=pltpu.CompilerParams(vmem_limit_bytes=56 * 2**20),
        name="attend_decode",
    )(ids, counts, stain, q, kv, kv, wo, tokens, stain_gain[:, None, :], stain_weight)


def per_device(
    tokens, enc_gain, w_query, w_key, w_value, w_out, neighbours, counts, stain_of_section, stain_gain, stain_weight
):
    q, kv, wo = project(tokens, enc_gain[None, :], w_query, w_key, w_value, w_out)
    seq = lax.axis_index("seq")
    blocks = TOK // BLOCK
    owner = neighbours // blocks - seq
    chip_side = 2 * (seq % 2) - 1
    part = jnp.where(owner == 0, 0, jnp.where(owner == chip_side, 1, 2))
    ids = part * blocks + neighbours % blocks
    return attention(ids, counts, stain_of_section, q, kv, wo, tokens, stain_gain, stain_weight)


def solution(mesh):
    placed = (
        P("seq", None),
        P(),
        P(None, "section"),
        P(None, "section"),
        P(None, "section"),
        P("section", None),
        P("seq", None),
        P("seq"),
        P("section"),
        P(),
        P(),
    )
    return jax.shard_map(
        per_device, mesh=mesh, in_specs=placed, out_specs=P("section", "seq", None), check_vma=False
    )
```

time: 283 us -> 127 us (0.45)
  waiting for transfers between devices: 137 us -> 0 us
  Pallas kernels: 0 us -> 120 us
  local copies, waits for them, and re-layouts: 76 us -> 5.13 us
  matrix products: 33.3 us -> 0 us
  between operations: 14.2 us -> 0.67 us
  starting transfers between devices: 12.1 us -> 0 us
  other arithmetic: 9.01 us -> 1.29 us
    pallas_call x0 -> x2, Pallas kernels: none -> 120 us  [the longest x1 84.8 us: project(): pl.pallas_call(gather_project, out_shape=[jax.ShapeDtypeStruct((GROUP, TO...]
    psum x1 -> x0, waiting for transfers between devices: 110 us -> none  [per_device(): lax.psum(partial_value.astype(jnp.bfloat16), 'section').astype(jnp.float32)]
    gather x2 -> x0, local copies, waits for them, and re-layouts: 31.1 us -> none  [per_device(): stored[:, local_ids]]
    ppermute x2 -> x0, waiting for transfers between devices: 27.1 us -> none  [the longest x1 20.4 us: with_halo(): lax.ppermute(head, axis, [((i + 1) % count, i) for i in range(ends)])]
    dot_general x6 -> x0, matrix products: 22.6 us -> none  [the longest x1 10.1 us: per_device(): jnp.einsum('nhqk,nkhd->nqhd', weights, picked[1], preferred_element_type=...]
    reshape x3 -> x0, local copies, waits for them, and re-layouts: 22.5 us -> none  [the longest x2 19.7 us: per_device(): stored = widened.reshape(2, 3 * local_blocks, BLOCK, local_heads, HEAD_DIM)]
    squeeze x2 -> x0, local copies, waits for them, and re-layouts: 14.6 us -> none  [the longest x1 7.32 us: per_device(): picked[0]]
    ppermute x2 -> x0, starting transfers between devices: 12.1 us -> none  [the longest x1 10.2 us: with_halo(): lax.ppermute(tail, axis, [(i, (i + 1) % count) for i in range(ends)])]
  transfers between devices with their start and end apart: 3 -> 0, of which waited for: 3 -> 0; matrix products, arithmetic and copies ran while one was open for 2% -> 0% of each run, Pallas kernels for 0% -> 0%
where the time goes in v1:
time: 127 us
  Pallas kernels  120 us (94%)
  local copies, waits for them, and re-layouts  5.13 us (4%)
  other arithmetic  1.29 us (1%)
    pallas_call x1, Pallas kernels, project(): pl.pallas_call(gather_project, out_shape=[jax.ShapeDtypeStruct((GROUP, TO...  84.8 us
    pallas_call x1, Pallas kernels, attention(): pl.pallas_call(attend_decode, out_shape=jax.ShapeDtypeStruct((1, TOK, PIX...  34.8 us
    unnamed x8, local copies, waits for them, and re-layouts  3.81 us

profile of v1, /device:TPU:1, one launch (start us, length us, event | category | flops | bytes accessed | tf_op | source)
XLA Modules:
  0.0 126.8 jit_solution(14027548477771320242)
XLA Ops:
  0.7 1.3 %fusion.1.ids_ref = s32[8,8]{1,0:T(8,128)} fusion(s32[8,8]{1,0:T(8,128)} %param.17, s32[]{:T(128)S(6)} %sub.18, s32[]{:T(128)S(6)} %axis_index.12), kind=kLoop, calls=%fused_computation.6 | loop fusion | flops 1664 | bytes 520 | tf_op jit(solution)/shard_map/add | solution.py:488
  1.9 1.3 %broadcast_in_dim.16.gain_ref = f32[3,1,1024]{2,1,0:T(1,128)} reshape(f32[3,1024]{1,0:T(4,128)} %param.20) | data formatting | bytes 24576 | tf_op jit(solution)/shard_map/broadcast_in_dim | solution.py:476
  3.3 0.0 copy-start
  3.3 1.0 copy-done
  4.3 0.0 copy-start.1
  4.3 1.0 copy-done.1
  5.4 0.0 copy-start.2
  5.4 1.0 copy-done.2
  6.4 0.0 copy-start.3
  6.4 0.7 copy-done.3
  7.1 84.8 %gather_project.1 = (bf16[4,1024,256]{2,1,0:T(8,128)(2,1)}, bf16[2,4,3072,256]{3,2,1,0:T(8,128)(2,1)}, bf16[4,1024,256]{2,1,0:T(8,128)(2,1)}) custom-call(bf16[1024,1024]{1,0:T(8,128)(2,1)} %tok_ref.1, f32[1,1024]{1,0:T(1,128)S(1)} %bitcast.1, bf16[1024,256]{1,0:T(8,128)(2,1)S(1)} %copy-done, bf16[1024,256]{1,0:T(8,128)(2,1)S(1)} %copy-done.1, ...), custom_call_target="tpu_custom_call" | custom-call | tf_op jit(solution)/shard_map/gather_project/pallas_call | solution.py:362
  91.9 34.8 %attend_decode.1 = bf16[1,1024,768]{2,1,0:T(8,128)(2,1)} custom-call(s32[8,8]{1,0:T(8,128)} %fusion.1.ids_ref, s32[8]{0:T(128)} %counts_ref.1, s32[1]{0:T(128)S(6)} %copy.12.stain_ref, bf16[4,1024,256]{2,1,0:T(8,128)(2,1)} %get-tuple-element.8.q_ref, bf16[2,4,3072,256]{3,2,1,0:T(8,128)(2,1)} %get-tuple-element.9.k_ref.v_ref, ...), custom_call_target="tpu_custom_call" | custom-call | tf_op jit(solution)/shard_map/attend_decode/pallas_call | solution.py:453
Async XLA Ops:
  3.3 1.0 copy-start
  4.3 1.0 copy-start.1
  5.4 1.0 copy-start.2
  6.4 0.7 copy-start.3

commit v2 on v1

--- a/solution.py
+++ b/solution.py
@@ -15,10 +15,12 @@
 PIX = 768
 GROUP = 4
 COLS = WIDTH // GROUP
-CHUNK = 32
+CHUNK = 16
 HALF = TOK // 2
 CHUNKS = HALF // CHUNK
-STEPS = CHUNKS + GROUP - 1
+SKEW = 5
+AHEAD = 6
+STEPS = CHUNKS + SKEW * (GROUP - 1)
 QSCALE = 0.125 * 1.4426950408889634
 
 F32 = jnp.float32
@@ -27,10 +29,10 @@
 
 
 def gather_project(
-    tok_hbm, gain_ref, wq_hbm, wk_hbm, wv_hbm, wo_hbm,
+    tok_hbm, gain_hbm, wq_hbm, wk_hbm, wv_hbm, wo_hbm,
     q_out, kv_out, wo_out,
-    raw, norm, wts, q_buf, own_kv, halo_kv,
-    tok_sem, wload_sem, lo_send, lo_recv, hi_send, hi_recv,
+    gain_buf, raw, norm, wts, q_buf, own_kv, halo_kv,
+    gain_sem, tok_sem, wload_sem, lo_send, lo_recv, hi_send, hi_recv,
     z_send, z_recv, row_send, row_recv, col_send, col_recv, pair_send, pair_recv,
     kv_send, kv_recv, store_sem, hstore_sem,
 ):
@@ -60,13 +62,13 @@
     last = jnp.where(sec == 3, 1, 0)
     lo_to = ((sec + 3) % 4, jnp.where(sec == 0, partner, seq))
     hi_to = ((sec + 1) % 4, jnp.where(sec == 3, partner, seq))
-    row_to = [(sec, seq_at((u + d) % 4, v)) for d in (1, 3, 2)]
+    row_to = [(sec, seq_at((u + d) % 4, v)) for d in (1, 3)]
     col_to = [(sec, seq_at(u, (v + d) % 4)) for d in (1, 3)]
 
     tok_loads = []
     for i in range(4):
         rows = pl.ds(i * 256, 256)
-        tok_loads.append(pltpu.make_async_copy(tok_hbm.at[rows, :], raw.at[rows, :], tok_sem.at[i]))
+        tok_loads.append(pltpu.make_async_copy(tok_hbm.at[rows, :], raw.at[0, rows, :], tok_sem.at[i]))
     w_loads = [
         pltpu.make_async_copy(src, wts.at[0, i], wload_sem.at[i])
         for i, src in enumerate((wq_hbm, wk_hbm, wv_hbm))
@@ -79,7 +81,8 @@
                 wload_sem.at[3 + i],
             )
         )
-    for copy in tok_loads + w_loads:
+    gain_load = pltpu.make_async_copy(gain_hbm, gain_buf, gain_sem)
+    for copy in [gain_load] + tok_loads + w_loads:
         copy.start()
 
     barrier = pltpu.get_barrier_semaphore()
@@ -87,19 +90,22 @@
     for peer in peers:
         pl.semaphore_signal(barrier, inc=1, device_id=peer, device_id_type=MESH)
 
-    gain = gain_ref[...]
-    for i in range(4):
-        tok_loads[i].wait()
-
-        def norm_rows(t, _):
-            rows = pl.ds(pl.multiple_of(i * 256 + t * 128, 128), 128)
-            x = raw[rows, :].astype(F32)
-            scale = lax.rsqrt(jnp.mean(x * x, axis=-1, keepdims=True) + 1e-05)
-            norm[0, rows, :] = (x * scale * gain).astype(BF16)
-            return 0
-
-        lax.fori_loop(0, 2, norm_rows, 0)
-
+    def norm_rows(i, start):
+        rows = pl.ds(pl.multiple_of(start, 128), 128)
+        x = raw[i, rows, :].astype(F32)
+        scale = lax.rsqrt(jnp.mean(x * x, axis=-1, keepdims=True) + 1e-05)
+        norm[i, rows, :] = (x * scale * gain_buf[...]).astype(BF16)
+
+    def norm_own(t, _):
+        norm_rows(0, t * 128)
+        return 0
+
+    def norm_halo(m):
+        norm_rows(1, m * 128)
+        norm_rows(1, HALF + m * 128)
+
+    for copy in w_loads + tok_loads:
+        copy.wait()
     pl.semaphore_wait(barrier, len(peers))
 
     def remote(src, dst, send, recv, to):
@@ -109,11 +115,11 @@
 
     def lo_copy(j):
         rows = pl.ds(pl.multiple_of(j * CHUNK, CHUNK), CHUNK)
-        return remote(norm.at[1 - first, rows, :], norm.at[1, rows, :], lo_send.at[j], lo_recv.at[j], lo_to)
+        return remote(raw.at[1 - first, rows, :], raw.at[1, rows, :], lo_send.at[j], lo_recv.at[j], lo_to)
 
     def hi_copy(j):
         rows = pl.ds(pl.multiple_of(HALF + j * CHUNK, CHUNK), CHUNK)
-        return remote(norm.at[1 - last, rows, :], norm.at[1, rows, :], hi_send.at[j], hi_recv.at[j], hi_to)
+        return remote(raw.at[1 - last, rows, :], raw.at[1, rows, :], hi_send.at[j], hi_recv.at[j], hi_to)
 
     def start_lo(j, _):
         lo_copy(j).start()
@@ -140,21 +146,28 @@
         remote(wts.at[0, 3, piece, :], wts.at[r + 1, 3, piece, :], z_send.at[3 + r], z_recv.at[3 + r], z_to[r])
         for r in range(3)
     ]
-    for copy in w_loads:
-        copy.wait()
     for copy in z_copies:
         copy.start()
 
     @pl.when(sec == 0)
     def _():
-        lax.fori_loop(0, CHUNKS, start_lo, 0)
+        lax.fori_loop(0, AHEAD, start_lo, 0)
 
     @pl.when(sec == 3)
     def _():
-        lax.fori_loop(0, CHUNKS, start_hi, 0)
+        lax.fori_loop(0, AHEAD, start_hi, 0)
+
+    def piece_rows(u1, start=0, size=32):
+        return pl.ds(pl.multiple_of(core * HALF + (v * 4 + u1) * 32 + start, 16), size)
 
     def row_copy(g, d):
-        return remote(slab(g, piece), slab(g, piece), row_send.at[g * 3 + d], row_recv.at[g * 3 + d], row_to[d])
+        if d < 2:
+            rows = piece_rows(u)
+        elif d == 2:
+            rows = piece_rows((u + 3) % 4, 0, 16)
+        else:
+            rows = piece_rows((u + 1) % 4, 16, 16)
+        return remote(slab(g, rows), slab(g, rows), row_send.at[g * 4 + d], row_recv.at[g * 4 + d], row_to[d % 2])
 
     def set_rows(v1, start=0, size=128):
         return pl.ds(pl.multiple_of(core * HALF + v1 * 128 + start, 32), size)
@@ -178,12 +191,17 @@
         else:
             for r in range(3):
                 z_copies[3 + r].wait_recv()
-        for d in range(3):
+        for d in range(2):
             row_copy(g, d).start()
 
+    def e2(g):
+        for d in range(2):
+            row_copy(g, d).wait_recv()
+            row_copy(g, 2 + d).start()
+
     def e3(g):
-        for d in range(3):
-            row_copy(g, d).wait_recv()
+        for d in range(2):
+            row_copy(g, 2 + d).wait_recv()
         for d in range(2):
             col_copy(g, d).start()
         pair_copy(g, 0).start()
@@ -206,7 +224,15 @@
             pair_copy(g, d).wait_recv()
 
     def halo_step(k):
-        j = k - 3 + sec
+        @pl.when((sec == 0) & (k + AHEAD < CHUNKS))
+        def _():
+            lo_copy(k + AHEAD).start()
+
+        @pl.when((sec == 3) & (k + AHEAD < CHUNKS))
+        def _():
+            hi_copy(k + AHEAD).start()
+
+        j = k - SKEW * (3 - sec)
 
         @pl.when((j >= 0) & (j < CHUNKS))
         def _():
@@ -216,7 +242,7 @@
             def _():
                 lo_copy(j).start()
 
-        i = k - sec
+        i = k - SKEW * sec
 
         @pl.when((i >= 0) & (i < CHUNKS))
         def _():
@@ -286,38 +312,57 @@
 
         return go
 
-    run(0, 3, [(1, seqn((e1, 0), (e1, 1))), (2, seqn((e1, 2), (e1, 3))), (3, seqn((e3, 0)))], lambda k: own_unit(0, k))
+    gain_load.wait()
+    lax.fori_loop(0, TOK // 128, norm_own, 0)
+
+    def unit_r0(k):
+        @pl.when(k % 2 == 0)
+        def _():
+            own_unit(0, k // 2)
+
+    run(0, 7, [(6, seqn((e1, 0), (e1, 1))), (7, seqn((e1, 2), (e1, 3)))], unit_r0)
     finish_own(0)
-    run(4, 6, [(4, seqn((e3, 1), (e3, 2))), (5, seqn((e3, 3), (e4, 0))), (6, seqn((e5, 0)))], lambda k: None)
-
-    def unit_r1(k):
-        own_unit(1, k - 7)
-
-        @pl.when(k < 9)
+    run(
+        8,
+        27,
+        [
+            (10, seqn((e2, 0), (e2, 1))),
+            (11, seqn((e2, 2))),
+            (12, seqn((e2, 3))),
+            (14, seqn((e3, 0))),
+            (15, seqn((e3, 1))),
+            (20, seqn((e4, 0), (e3, 2))),
+            (23, seqn((e4, 1), (e3, 3))),
+            (24, seqn((e5, 0))),
+            (25, seqn((norm_halo, 0))),
+            (26, lambda: halo_unit(0, 0)),
+        ],
+        lambda k: None,
+    )
+    run(28, 32, [(28, seqn((e6, 0), (e4, 2))), (29, seqn((e5, 1))), (32, seqn((e6, 1), (e4, 3), (norm_halo, 1)))], lambda k: pl.when(k < 32)(lambda: own_unit(1, k - 28)))
+    finish_own(1)
+
+    def unit_r2(k):
+        t = k - 33
+        own_unit(2, t)
+
+        @pl.when(t < 3)
         def _():
-            halo_unit(0, k - 7)
-
-    run(7, 10, [(7, seqn((e6, 0))), (8, seqn((e4, 1))), (9, seqn((e5, 1)))], unit_r1)
-    finish_own(1)
-
-    def unit_r2(k):
-        own_unit(2, k - 11)
-        t = k - 11
-        halo_unit(1 - t // 3, t - t // 3)
-
-    run(11, 14, [(11, seqn((e6, 1), (e4, 2))), (12, seqn((e5, 2))), (13, seqn((e4, 3))), (14, seqn((e5, 3)))], unit_r2)
+            halo_unit((t + 1) // 2, (t + 1) % 2)
+
+    run(33, 36, [(34, seqn((e5, 2)))], unit_r2)
     finish_own(2)
-
-    def unit_r3(k):
-        own_unit(3, k - 15)
-        halo_unit(2, k - 15)
-
-        @pl.when(k < 17)
-        def _():
-            halo_unit(k - 15, 3)
-
-    run(15, STEPS - 1, [(15, seqn((e6, 2))), (16, seqn((e6, 3)))], unit_r3)
+    run(37, 40, [(37, seqn((e6, 2))), (38, seqn((e5, 3)))], lambda k: own_unit(3, k - 37))
     finish_own(3)
+
+    def unit_halo(k):
+        t = k - 41
+        halo_unit(jnp.where(t < 4, t % 2, 2), jnp.where(t < 4, 2 + t // 2, t - 4))
+
+    run(41, STEPS - 1, [(42, seqn((norm_halo, 2))), (44, seqn((e6, 3)))], unit_halo)
+    halo_unit(2, 2)
+    halo_unit(2, 3)
+    norm_halo(3)
     wo_store = pltpu.make_async_copy(wts.at[:, 3], wo_out, wload_sem.at[7])
     wo_store.start()
     for m in range(3):
@@ -341,9 +386,8 @@
     for copy in z_copies:
         copy.wait_send()
     for g in range(4):
-        for d in range(3):
+        for d in range(4):
             row_copy(g, d).wait_send()
-        for d in range(4):
             col_copy(g, d).wait_send()
             pair_copy(g, d).wait_send()
     for r in range(GROUP):
@@ -357,7 +401,7 @@
 
 
 def project(tokens, gain, wq, wk, wv, wo):
-    any_spec = pl.BlockSpec(memory_space=pl.ANY)
+    any_spec = pl.BlockSpec(memory_space=pltpu.HBM)
     dma = pltpu.SemaphoreType.DMA
     return pl.pallas_call(
         gather_project,
@@ -366,22 +410,23 @@
             jax.ShapeDtypeStruct((2, GROUP, 3 * TOK, COLS), BF16),
             jax.ShapeDtypeStruct((GROUP, WIDTH, COLS), BF16),
         ],
-        in_specs=[any_spec, pl.BlockSpec(memory_space=pltpu.VMEM)] + [any_spec] * 4,
+        in_specs=[any_spec] * 6,
         out_specs=[any_spec] * 3,
         scratch_shapes=[
-            pltpu.VMEM((TOK, WIDTH), BF16),
+            pltpu.VMEM((1, WIDTH), F32),
+            pltpu.VMEM((2, TOK, WIDTH), BF16),
             pltpu.VMEM((2, TOK, WIDTH), BF16),
             pltpu.VMEM((GROUP, 4, WIDTH, COLS), BF16),
             pltpu.VMEM((GROUP, TOK, COLS), BF16),
             pltpu.VMEM((GROUP, 2, TOK, COLS), BF16),
             pltpu.VMEM((2, GROUP, TOK, COLS), BF16),
-            dma((4,)), dma((8,)),
+            dma, dma((4,)), dma((8,)),
             dma((CHUNKS,)), dma((CHUNKS,)), dma((CHUNKS,)), dma((CHUNKS,)),
-            dma((6,)), dma((6,)), dma((12,)), dma((12,)), dma((16,)), dma((16,)), dma((16,)), dma((16,)),
+            dma((6,)), dma((6,)), dma((16,)), dma((16,)), dma((16,)), dma((16,)), dma((16,)), dma((16,)),
             dma((4,)), dma((4,)), dma((8,)), dma((8,)),
         ],
         compiler_params=pltpu.CompilerParams(
-            collective_id=0, has_side_effects=True, vmem_limit_bytes=52 * 2**20
+            collective_id=0, has_side_effects=True, vmem_limit_bytes=62 * 2**20
         ),
         name="gather_project",
     )(tokens, gain, wq, wk, wv, wo)
@@ -391,17 +436,24 @@
 
 
 def attend_decode(
-    ids_ref, counts_ref, stain_ref,
+    near_ref, counts_ref, stain_ref,
     q_ref, k_ref, v_ref, wo_ref, tok_ref, gain_ref, sw_ref,
     out_ref, att, e_scr,
 ):
-    del stain_ref
     step = pl.program_id(0)
+    seq = lax.axis_index("seq")
+    blocks = TOK // BLOCK
+
+    def place(near):
+        owner = near // blocks - seq
+        part = jnp.where(owner == 0, 0, jnp.where(owner == 2 * (seq % 2) - 1, 1, 2))
+        return pl.multiple_of((part * blocks + near % blocks) * BLOCK, BLOCK)
+
     lane = lax.broadcasted_iota(jnp.int32, (BLOCK, BLOCK), 1)
 
     def block(i, _):
         rows = pl.ds(pl.multiple_of(i * BLOCK, BLOCK), BLOCK)
-        starts = [pl.multiple_of(ids_ref[i, j] * BLOCK, BLOCK) for j in range(NEIGH)]
+        starts = [place(near_ref[i, j]) for j in range(NEIGH)]
 
         def run(n):
             for p in range(PAIRS):
@@ -429,7 +481,7 @@
 
     @pl.when(step == GROUP // 2 - 1)
     def _():
-        gain = gain_ref[0]
+        gain = gain_ref[pl.ds(stain_ref[0], 1), :]
 
         def rows_out(t, _):
             rows = pl.ds(pl.multiple_of(t * 256, 256), 256)
@@ -448,7 +500,7 @@
         lax.fori_loop(0, 4, rows_out, 0)
 
 
-def attention(ids, counts, stain, q, kv, wo, tokens, stain_gain, stain_weight):
+def attention(neighbours, counts, stain, q, kv, wo, tokens, stain_gain, stain_weight):
     half = GROUP // 2
     return pl.pallas_call(
         attend_decode,
@@ -462,8 +514,8 @@
                 pl.BlockSpec((1, half, 3 * TOK, COLS), lambda g, *_: (1, g, 0, 0)),
                 pl.BlockSpec((GROUP, WIDTH, COLS), lambda g, *_: (0, 0, 0), pipeline_mode=pl.Buffered(1)),
                 pl.BlockSpec((TOK, WIDTH), lambda g, *_: (0, 0), pipeline_mode=pl.Buffered(1)),
-                pl.BlockSpec((1, 1, WIDTH), lambda g, ids, counts, stain: (stain[0], 0, 0)),
-                pl.BlockSpec((1, WIDTH, PIX), lambda g, ids, counts, stain: (stain[0], 0, 0), pipeline_mode=pl.Buffered(1)),
+                pl.BlockSpec(memory_space=pltpu.VMEM),
+                pl.BlockSpec((1, WIDTH, PIX), lambda g, near, counts, stain: (stain[0], 0, 0), pipeline_mode=pl.Buffered(1)),
             ],
             out_specs=pl.BlockSpec((1, TOK, PIX), lambda g, *_: (0, 0, 0)),
             scratch_shapes=[
@@ -473,20 +525,14 @@
         ),
         compiler_params=pltpu.CompilerParams(vmem_limit_bytes=56 * 2**20),
         name="attend_decode",
-    )(ids, counts, stain, q, kv, kv, wo, tokens, stain_gain[:, None, :], stain_weight)
+    )(neighbours, counts, stain, q, kv, kv, wo, tokens, stain_gain, stain_weight)
 
 
 def per_device(
     tokens, enc_gain, w_query, w_key, w_value, w_out, neighbours, counts, stain_of_section, stain_gain, stain_weight
 ):
     q, kv, wo = project(tokens, enc_gain[None, :], w_query, w_key, w_value, w_out)
-    seq = lax.axis_index("seq")
-    blocks = TOK // BLOCK
-    owner = neighbours // blocks - seq
-    chip_side = 2 * (seq % 2) - 1
-    part = jnp.where(owner == 0, 0, jnp.where(owner == chip_side, 1, 2))
-    ids = part * blocks + neighbours % blocks
-    return attention(ids, counts, stain_of_section, q, kv, wo, tokens, stain_gain, stain_weight)
+    return attention(neighbours, counts, stain_of_section, q, kv, wo, tokens, stain_gain, stain_weight)
 
 
 def solution(mesh):

time: 127 us -> 96.5 us (0.76); the launches traced: 127 us -> 94.8 us
  Pallas kernels: 120 us -> 94.2 us
  local copies, waits for them, and re-layouts: 5.13 us -> 0 us
  other arithmetic: 1.29 us -> 0 us
    pallas_call x1, Pallas kernels: 84.8 us -> 60.6 us  [project(): pl.pallas_call(gather_project, out_shape=[jax.ShapeDtypeStruct((GROUP, TO...]
    unnamed x8 -> x0, local copies, waits for them, and re-layouts: 3.81 us -> none
    broadcast_in_dim x1 -> x0, local copies, waits for them, and re-layouts: 1.32 us -> none  [attention(): stain_gain[:, None, :]]
    add x1 -> x0, other arithmetic: 1.29 us -> none  [per_device(): ids = part * blocks + neighbours % blocks]
where the time goes in v2:
time: 96.5 us; the launch traced here: 94.8 us
  Pallas kernels  94.2 us (98%)
    pallas_call x1, Pallas kernels, project(): pl.pallas_call(gather_project, out_shape=[jax.ShapeDtypeStruct((GROUP, TO...  60.6 us
    pallas_call x1, Pallas kernels, attention(): pl.pallas_call(attend_decode, out_shape=jax.ShapeDtypeStruct((1, TOK, PIX...  33.6 us

profile of v2, /device:TPU:1, one launch (start us, length us, event | category | flops | bytes accessed | tf_op | source)
XLA Modules:
  0.0 94.8 jit_solution(249749255498717242)
XLA Ops:
  0.7 60.6 %gather_project.1 = (bf16[4,1024,256]{2,1,0:T(8,128)(2,1)}, bf16[2,4,3072,256]{3,2,1,0:T(8,128)(2,1)}, bf16[4,1024,256]{2,1,0:T(8,128)(2,1)}) custom-call(bf16[1024,1024]{1,0:T(8,128)(2,1)} %tok_ref.1, f32[1,1024]{1,0:T(1,128)} %bitcast.1, bf16[1024,256]{1,0:T(8,128)(2,1)} %wq_hbm.1, bf16[1024,256]{1,0:T(8,128)(2,1)} %wk_hbm.1, bf16[1024,256]{1,0:T(8,128)(2,1)} %wv_hbm.1, ...), custom_call_target="tpu_custom_call" | custom-call | tf_op jit(solution)/shard_map/gather_project/pallas_call | solution.py:406
  61.2 33.6 %attend_decode.1 = bf16[1,1024,768]{2,1,0:T(8,128)(2,1)} custom-call(s32[8,8]{1,0:T(8,128)} %near_ref.1, s32[8]{0:T(128)} %counts_ref.1, s32[1]{0:T(128)S(6)} %copy.12.stain_ref, bf16[4,1024,256]{2,1,0:T(8,128)(2,1)} %get-tuple-element.8.q_ref, bf16[2,4,3072,256]{3,2,1,0:T(8,128)(2,1)} %get-tuple-element.9.k_ref.v_ref, ...), custom_call_target="tpu_custom_call" | custom-call | tf_op jit(solution)/shard_map/attend_decode/pallas_call | solution.py:505

commit v3 on v2

--- a/solution.py
+++ b/solution.py
@@ -253,21 +253,26 @@
                 hi_copy(i).start()
 
     def own_unit(r, t):
-        rows = pl.ds(pl.multiple_of(t * 256, 256), 256)
+        rows = pl.ds(pl.multiple_of(t * 512, 512), 512)
         x = norm[0, rows, :]
         q = jnp.dot(x, wts[r, 0], preferred_element_type=F32)
         q_buf[r, rows, :] = (q * QSCALE).astype(BF16)
         own_kv[r, 0, rows, :] = jnp.dot(x, wts[r, 1], preferred_element_type=F32).astype(BF16)
         own_kv[r, 1, rows, :] = jnp.dot(x, wts[r, 2], preferred_element_type=F32).astype(BF16)
 
-    def halo_unit(m, r):
-        low = pl.ds(pl.multiple_of(m * 128, 128), 128)
-        high = pl.ds(pl.multiple_of(HALF + m * 128, 128), 128)
+    def halo_unit(m, count, r):
+        size = 128 * count
+        low = pl.ds(m * 128, size)
+        high = pl.ds(HALF + m * 128, size)
         x = jnp.concatenate([norm[1, low, :], norm[1, high, :]], axis=0)
         for w in range(2):
             y = jnp.dot(x, wts[r, 1 + w], preferred_element_type=F32).astype(BF16)
-            halo_kv[w, r, low, :] = y[:128]
-            halo_kv[w, r, high, :] = y[128:]
+            halo_kv[w, r, low, :] = y[:size]
+            halo_kv[w, r, high, :] = y[size:]
+
+    def halo_all(m):
+        for r in range(GROUP):
+            halo_unit(m, 1, r)
 
     def own_stores(r):
         return [
@@ -316,9 +321,9 @@
     lax.fori_loop(0, TOK // 128, norm_own, 0)
 
     def unit_r0(k):
-        @pl.when(k % 2 == 0)
+        @pl.when(k % 4 == 0)
         def _():
-            own_unit(0, k // 2)
+            own_unit(0, k // 4)
 
     run(0, 7, [(6, seqn((e1, 0), (e1, 1))), (7, seqn((e1, 2), (e1, 3)))], unit_r0)
     finish_own(0)
@@ -335,33 +340,39 @@
             (23, seqn((e4, 1), (e3, 3))),
             (24, seqn((e5, 0))),
             (25, seqn((norm_halo, 0))),
-            (26, lambda: halo_unit(0, 0)),
         ],
         lambda k: None,
     )
-    run(28, 32, [(28, seqn((e6, 0), (e4, 2))), (29, seqn((e5, 1))), (32, seqn((e6, 1), (e4, 3), (norm_halo, 1)))], lambda k: pl.when(k < 32)(lambda: own_unit(1, k - 28)))
+    run(28, 32, [(28, seqn((e6, 0), (e4, 2))), (29, seqn((e5, 1))), (32, seqn((e6, 1), (e4, 3), (norm_halo, 1)))], lambda k: pl.when((k == 28) | (k == 30))(lambda: own_unit(1, (k - 28) // 2)))
     finish_own(1)
 
     def unit_r2(k):
         t = k - 33
-        own_unit(2, t)
-
-        @pl.when(t < 3)
+
+        @pl.when(t % 2 == 0)
         def _():
-            halo_unit((t + 1) // 2, (t + 1) % 2)
+            own_unit(2, t // 2)
+            halo_unit(0, 2, t // 2)
 
     run(33, 36, [(34, seqn((e5, 2)))], unit_r2)
     finish_own(2)
-    run(37, 40, [(37, seqn((e6, 2))), (38, seqn((e5, 3)))], lambda k: own_unit(3, k - 37))
+
+    def unit_r3(k):
+        t = k - 37
+
+        @pl.when(t % 2 == 0)
+        def _():
+            own_unit(3, t // 2)
+            halo_unit(0, 2, 2 + t // 2)
+
+    run(37, 40, [(37, seqn((e6, 2))), (38, seqn((e5, 3)))], unit_r3)
     finish_own(3)
-
-    def unit_halo(k):
-        t = k - 41
-        halo_unit(jnp.where(t < 4, t % 2, 2), jnp.where(t < 4, 2 + t // 2, t - 4))
-
-    run(41, STEPS - 1, [(42, seqn((norm_halo, 2))), (44, seqn((e6, 3)))], unit_halo)
-    halo_unit(2, 2)
-    halo_unit(2, 3)
+    run(
+        41,
+        STEPS - 1,
+        [(42, seqn((norm_halo, 2))), (43, seqn((e6, 3)))],
+        lambda k: pl.when(k == 43)(lambda: halo_all(2)),
+    )
     norm_halo(3)
     wo_store = pltpu.make_async_copy(wts.at[:, 3], wo_out, wload_sem.at[7])
     wo_store.start()
@@ -369,11 +380,7 @@
         for copy in halo_stores(m):
             copy.start()
 
-    def tail(r, _):
-        halo_unit(3, r)
-        return 0
-
-    lax.fori_loop(0, GROUP, tail, 0)
+    halo_all(3)
     for copy in halo_stores(3):
         copy.start()
 
@@ -433,16 +440,37 @@
 
 
 PAIRS = 4
+LAG = 4
+ROWS = 512
 
 
 def attend_decode(
-    near_ref, counts_ref, stain_ref,
-    q_ref, k_ref, v_ref, wo_ref, tok_ref, gain_ref, sw_ref,
-    out_ref, att, e_scr,
+    near_ref, counts_ref, stain_ref, q_hbm, kv_hbm, wo_hbm, tok_hbm, gain_ref, sw_hbm,
+    out_hbm,
+    q_buf, k_buf, v_buf, wo_buf, tok_buf, sw_buf, att, e_scr, out_buf,
+    q_sem, k_sem, v_sem, late_sem, out_sem,
 ):
-    step = pl.program_id(0)
     seq = lax.axis_index("seq")
     blocks = TOK // BLOCK
+    stain = stain_ref[0]
+
+    def loads(r):
+        return [
+            pltpu.make_async_copy(q_hbm.at[r], q_buf.at[r], q_sem.at[r]),
+            pltpu.make_async_copy(kv_hbm.at[0, r], k_buf.at[r], k_sem.at[r]),
+            pltpu.make_async_copy(kv_hbm.at[1, r], v_buf.at[r], v_sem.at[r]),
+        ]
+
+    late = [
+        pltpu.make_async_copy(wo_hbm, wo_buf, late_sem.at[0]),
+        pltpu.make_async_copy(tok_hbm, tok_buf, late_sem.at[1]),
+        pltpu.make_async_copy(sw_hbm.at[stain], sw_buf, late_sem.at[2]),
+    ]
+    for r in range(GROUP):
+        for copy in loads(r):
+            copy.start()
+    for copy in late:
+        copy.start()
 
     def place(near):
         owner = near // blocks - seq
@@ -451,81 +479,104 @@
 
     lane = lax.broadcasted_iota(jnp.int32, (BLOCK, BLOCK), 1)
 
-    def block(i, _):
+    def block(i, h):
         rows = pl.ds(pl.multiple_of(i * BLOCK, BLOCK), BLOCK)
         starts = [place(near_ref[i, j]) for j in range(NEIGH)]
 
+        def score(p, n):
+            r, c = 2 * h + p // 2, (p % 2) * BLOCK
+            q = q_buf[r, rows, c : c + BLOCK]
+            zero = jnp.zeros_like(q)
+            both = jnp.concatenate([jnp.where(lane < HEAD_DIM, q, zero), jnp.where(lane < HEAD_DIM, zero, q)], axis=0)
+            k = jnp.concatenate([k_buf[r, pl.ds(starts[j], BLOCK), c : c + BLOCK] for j in range(n)], axis=0)
+            s = lax.dot_general(both, k, (((1,), (1,)), ((), ())), preferred_element_type=F32)
+            top = jnp.max(s, axis=1, keepdims=True)
+            e_scr[p, :, : n * BLOCK] = jnp.exp2(s - top).astype(BF16)
+
+        def mix(p, n):
+            r, c = 2 * h + p // 2, (p % 2) * BLOCK
+            v = jnp.concatenate([v_buf[r, pl.ds(starts[j], BLOCK), c : c + BLOCK] for j in range(n)], axis=0)
+            v = jnp.concatenate([v, jnp.ones((n * BLOCK, BLOCK), BF16)], axis=1)
+            o = jnp.dot(e_scr[p, :, : n * BLOCK], v, preferred_element_type=F32)
+            o = o[:, :BLOCK] / o[:, BLOCK:]
+            att[r, rows, c : c + BLOCK] = jnp.where(lane < HEAD_DIM, o[:BLOCK], o[BLOCK:]).astype(BF16)
+
         def run(n):
-            for p in range(PAIRS):
-                r, c = p // 2, (p % 2) * BLOCK
-                q = q_ref[r, rows, c : c + BLOCK]
-                zero = jnp.zeros_like(q)
-                both = jnp.concatenate([jnp.where(lane < HEAD_DIM, q, zero), jnp.where(lane < HEAD_DIM, zero, q)], axis=0)
-                k = jnp.concatenate([k_ref[0, r, pl.ds(starts[j], BLOCK), c : c + BLOCK] for j in range(n)], axis=0)
-                s = lax.dot_general(both, k, (((1,), (1,)), ((), ())), preferred_element_type=F32)
-                top = jnp.max(s, axis=1, keepdims=True)
-                e_scr[p, :, : n * BLOCK] = jnp.exp2(s - top).astype(BF16)
-            for p in range(PAIRS):
-                r, c = p // 2, (p % 2) * BLOCK
-                v = jnp.concatenate([v_ref[0, r, pl.ds(starts[j], BLOCK), c : c + BLOCK] for j in range(n)], axis=0)
-                v = jnp.concatenate([v, jnp.ones((n * BLOCK, BLOCK), BF16)], axis=1)
-                o = jnp.dot(e_scr[p, :, : n * BLOCK], v, preferred_element_type=F32)
-                o = o[:, :BLOCK] / o[:, BLOCK:]
-                att[step * 2 + r, rows, c : c + BLOCK] = jnp.where(lane < HEAD_DIM, o[:BLOCK], o[BLOCK:]).astype(BF16)
+            for t in range(PAIRS + LAG):
+                if t < PAIRS:
+                    score(t, n)
+                if t >= LAG:
+                    mix(t - LAG, n)
 
         for n in range(3, NEIGH + 1):
             pl.when(counts_ref[i] == n)(functools.partial(run, n))
+
+    def half(h, _):
+        for r in range(2):
+            for copy in loads(2 * h + r):
+                copy.wait()
+
+        def one(i, _):
+            block(i, h)
+            return 0
+
+        lax.fori_loop(0, blocks, one, 0)
         return 0
 
-    lax.fori_loop(0, TOK // BLOCK, block, 0)
-
-    @pl.when(step == GROUP // 2 - 1)
-    def _():
-        gain = gain_ref[pl.ds(stain_ref[0], 1), :]
-
-        def rows_out(t, _):
-            rows = pl.ds(pl.multiple_of(t * 256, 256), 256)
-            x = jnp.concatenate([att[r, rows, :] for r in range(GROUP)], axis=1)
-            parts = []
-            for c in range(GROUP):
-                w = jnp.concatenate([wo_ref[r, c * COLS : (c + 1) * COLS, :] for r in range(GROUP)], axis=0)
-                parts.append(jnp.dot(x, w, preferred_element_type=F32))
-            mixed = jnp.concatenate(parts, axis=1)
-            encoded = (tok_ref[rows, :].astype(F32) + mixed).astype(BF16).astype(F32)
-            scale = lax.rsqrt(jnp.mean(encoded * encoded, axis=-1, keepdims=True) + 1e-05)
-            decoded = (encoded * scale * gain).astype(BF16)
-            out_ref[0, rows, :] = jnp.dot(decoded, sw_ref[0], preferred_element_type=F32).astype(BF16)
-            return 0
-
-        lax.fori_loop(0, 4, rows_out, 0)
+    lax.fori_loop(0, GROUP // 2, half, 0)
+
+    for copy in late:
+        copy.wait()
+    gain = gain_ref[pl.ds(stain, 1), :]
+
+    def store(t):
+        rows = pl.ds(t * ROWS, ROWS)
+        return pltpu.make_async_copy(out_buf.at[rows, :], out_hbm.at[0, rows, :], out_sem.at[t])
+
+    def rows_out(t, _):
+        rows = pl.ds(pl.multiple_of(t * ROWS, ROWS), ROWS)
+        x = jnp.concatenate([att[r, rows, :] for r in range(GROUP)], axis=1)
+        parts = []
+        for c in range(GROUP):
+            w = jnp.concatenate([wo_buf[r, c * COLS : (c + 1) * COLS, :] for r in range(GROUP)], axis=0)
+            parts.append(jnp.dot(x, w, preferred_element_type=F32))
+        mixed = jnp.concatenate(parts, axis=1)
+        encoded = (tok_buf[rows, :].astype(F32) + mixed).astype(BF16).astype(F32)
+        scale = lax.rsqrt(jnp.mean(encoded * encoded, axis=-1, keepdims=True) + 1e-05)
+        decoded = (encoded * scale * gain).astype(BF16)
+        out_buf[rows, :] = jnp.dot(decoded, sw_buf[...], preferred_element_type=F32).astype(BF16)
+        store(t).start()
+        return 0
+
+    lax.fori_loop(0, TOK // ROWS, rows_out, 0)
+    for t in range(TOK // ROWS):
+        store(t).wait()
 
 
 def attention(neighbours, counts, stain, q, kv, wo, tokens, stain_gain, stain_weight):
-    half = GROUP // 2
+    hbm = pl.BlockSpec(memory_space=pltpu.HBM)
+    smem = pl.BlockSpec(memory_space=pltpu.SMEM)
+    dma = pltpu.SemaphoreType.DMA
     return pl.pallas_call(
         attend_decode,
         out_shape=jax.ShapeDtypeStruct((1, TOK, PIX), BF16),
-        grid_spec=pltpu.PrefetchScalarGridSpec(
-            num_scalar_prefetch=3,
-            grid=(2,),
-            in_specs=[
-                pl.BlockSpec((half, TOK, COLS), lambda g, *_: (g, 0, 0)),
-                pl.BlockSpec((1, half, 3 * TOK, COLS), lambda g, *_: (0, g, 0, 0)),
-                pl.BlockSpec((1, half, 3 * TOK, COLS), lambda g, *_: (1, g, 0, 0)),
-                pl.BlockSpec((GROUP, WIDTH, COLS), lambda g, *_: (0, 0, 0), pipeline_mode=pl.Buffered(1)),
-                pl.BlockSpec((TOK, WIDTH), lambda g, *_: (0, 0), pipeline_mode=pl.Buffered(1)),
-                pl.BlockSpec(memory_space=pltpu.VMEM),
-                pl.BlockSpec((1, WIDTH, PIX), lambda g, near, counts, stain: (stain[0], 0, 0), pipeline_mode=pl.Buffered(1)),
-            ],
-            out_specs=pl.BlockSpec((1, TOK, PIX), lambda g, *_: (0, 0, 0)),
-            scratch_shapes=[
-                pltpu.VMEM((GROUP, TOK, COLS), BF16),
-                pltpu.VMEM((PAIRS, 2 * BLOCK, NEIGH * BLOCK), BF16),
-            ],
-        ),
-        compiler_params=pltpu.CompilerParams(vmem_limit_bytes=56 * 2**20),
+        in_specs=[smem] * 3 + [hbm] * 4 + [pl.BlockSpec(memory_space=pltpu.VMEM), hbm],
+        out_specs=hbm,
+        scratch_shapes=[
+            pltpu.VMEM((GROUP, TOK, COLS), BF16),
+            pltpu.VMEM((GROUP, 3 * TOK, COLS), BF16),
+            pltpu.VMEM((GROUP, 3 * TOK, COLS), BF16),
+            pltpu.VMEM((GROUP, WIDTH, COLS), BF16),
+            pltpu.VMEM((TOK, WIDTH), BF16),
+            pltpu.VMEM((WIDTH, PIX), BF16),
+            pltpu.VMEM((GROUP, TOK, COLS), BF16),
+            pltpu.VMEM((PAIRS, 2 * BLOCK, NEIGH * BLOCK), BF16),
+            pltpu.VMEM((TOK, PIX), BF16),
+            dma((GROUP,)), dma((GROUP,)), dma((GROUP,)), dma((3,)), dma((TOK // ROWS,)),
+        ],
+        compiler_params=pltpu.CompilerParams(vmem_limit_bytes=62 * 2**20),
         name="attend_decode",
-    )(neighbours, counts, stain, q, kv, kv, wo, tokens, stain_gain, stain_weight)
+    )(neighbours, counts, stain, q, kv, wo, tokens, stain_gain, stain_weight)
 
 
 def per_device(

time: 96.5 us -> 91.2 us (0.945); the launches traced: 94.8 us -> 91 us
  Pallas kernels: 94.2 us -> 90.1 us
    pallas_call x1, Pallas kernels: 33.6 us -> 30.5 us  [attention(): pl.pallas_call(attend_decode, out_shape=jax.ShapeDtypeStruct((1, TOK, PIX...]
where the time goes in v3:
time: 91.2 us; the launch traced here: 91 us
  Pallas kernels  90.1 us (99%)
    pallas_call x1, Pallas kernels, project(): pl.pallas_call(gather_project, out_shape=[jax.ShapeDtypeStruct((GROUP, TO...  59.7 us
    pallas_call x1, Pallas kernels, attention(): pl.pallas_call(attend_decode, out_shape=jax.ShapeDtypeStruct((1, TOK, PIX...  30.5 us

profile of v3, /device:TPU:1, one launch (start us, length us, event | category | flops | bytes accessed | tf_op | source)
XLA Modules:
  0.0 91.0 jit_solution(16655082025842946960)
XLA Ops:
  0.7 59.7 %gather_project.1 = (bf16[4,1024,256]{2,1,0:T(8,128)(2,1)}, bf16[2,4,3072,256]{3,2,1,0:T(8,128)(2,1)}, bf16[4,1024,256]{2,1,0:T(8,128)(2,1)}) custom-call(bf16[1024,1024]{1,0:T(8,128)(2,1)} %tok_hbm.3, f32[1,1024]{1,0:T(1,128)} %bitcast.1, bf16[1024,256]{1,0:T(8,128)(2,1)} %wq_hbm.1, bf16[1024,256]{1,0:T(8,128)(2,1)} %wk_hbm.1, bf16[1024,256]{1,0:T(8,128)(2,1)} %wv_hbm.1, ...), custom_call_target="tpu_custom_call" | custom-call | tf_op jit(solution)/shard_map/gather_project/pallas_call | solution.py:413
  60.3 30.5 %attend_decode.1 = bf16[1,1024,768]{2,1,0:T(8,128)(2,1)} custom-call(s32[8,8]{1,0:T(8,128)} %near_ref.1, s32[8]{0:T(128)} %counts_ref.1, s32[1]{0:T(128)S(6)} %copy.12.stain_ref, bf16[4,1024,256]{2,1,0:T(8,128)(2,1)} %get-tuple-element.8.q_hbm, bf16[2,4,3072,256]{3,2,1,0:T(8,128)(2,1)} %get-tuple-element.9.kv_hbm, ...), custom_call_target="tpu_custom_call" | custom-call | tf_op jit(solution)/shard_map/attend_decode/pallas_call | solution.py:560

commit v4 on v3

--- a/solution.py
+++ b/solution.py
@@ -82,7 +82,7 @@
             )
         )
     gain_load = pltpu.make_async_copy(gain_hbm, gain_buf, gain_sem)
-    for copy in [gain_load] + tok_loads + w_loads:
+    for copy in w_loads + tok_loads + [gain_load]:
         copy.start()
 
     barrier = pltpu.get_barrier_semaphore()
@@ -104,7 +104,7 @@
         norm_rows(1, m * 128)
         norm_rows(1, HALF + m * 128)
 
-    for copy in w_loads + tok_loads:
+    for copy in w_loads:
         copy.wait()
     pl.semaphore_wait(barrier, len(peers))
 
@@ -148,6 +148,8 @@
     ]
     for copy in z_copies:
         copy.start()
+    for copy in tok_loads:
+        copy.wait()
 
     @pl.when(sec == 0)
     def _():
@@ -441,7 +443,7 @@
 
 PAIRS = 4
 LAG = 4
-ROWS = 512
+ROWS = 1024
 
 
 def attend_decode(

time: 91.2 us -> 91.4 us (level)
  no operation moved by 1% of the time
where the time goes in v4:
time: 91.4 us; the launch traced here: 90.3 us
  Pallas kernels  89.5 us (98%)
    pallas_call x1, Pallas kernels, project(): pl.pallas_call(gather_project, out_shape=[jax.ShapeDtypeStruct((GROUP, TO...  59.6 us
    pallas_call x1, Pallas kernels, attention(): pl.pallas_call(attend_decode, out_shape=jax.ShapeDtypeStruct((1, TOK, PIX...  29.9 us

profile of v4, /device:TPU:1, one launch (start us, length us, event | category | flops | bytes accessed | tf_op | source)
XLA Modules:
  0.0 90.3 jit_solution(11909878534433418654)
XLA Ops:
  0.7 59.6 %gather_project.1 = (bf16[4,1024,256]{2,1,0:T(8,128)(2,1)}, bf16[2,4,3072,256]{3,2,1,0:T(8,128)(2,1)}, bf16[4,1024,256]{2,1,0:T(8,128)(2,1)}) custom-call(bf16[1024,1024]{1,0:T(8,128)(2,1)} %tok_hbm.3, f32[1,1024]{1,0:T(1,128)} %bitcast.1, bf16[1024,256]{1,0:T(8,128)(2,1)} %wq_hbm.1, bf16[1024,256]{1,0:T(8,128)(2,1)} %wk_hbm.1, bf16[1024,256]{1,0:T(8,128)(2,1)} %wv_hbm.1, ...), custom_call_target="tpu_custom_call" | custom-call | tf_op jit(solution)/shard_map/gather_project/pallas_call | solution.py:415
  60.2 29.9 %attend_decode.1 = bf16[1,1024,768]{2,1,0:T(8,128)(2,1)} custom-call(s32[8,8]{1,0:T(8,128)} %near_ref.1, s32[8]{0:T(128)} %counts_ref.1, s32[1]{0:T(128)S(6)} %copy.12.stain_ref, bf16[4,1024,256]{2,1,0:T(8,128)(2,1)} %get-tuple-element.8.q_hbm, bf16[2,4,3072,256]{3,2,1,0:T(8,128)(2,1)} %get-tuple-element.9.kv_hbm, ...), custom_call_target="tpu_custom_call" | custom-call | tf_op jit(solution)/shard_map/attend_decode/pallas_call | solution.py:562
